TPU v7x, 32 devices: a whole 2x2x4 slice. The times are simulated.
32 devices in a mesh: dp: 4 (over x, core), context: 2 (over y), expert: 4 (over z).
Axes of the slice: x: 2, y: 2, z: 4, core: 2. Of those that a mesh axis runs over, the one named last changes fastest.
Arguments:
- tokens: bfloat16 [4, 1024, 768], P('dp', ('context', 'expert')), may hold values from -6 to 6
- w_query: bfloat16 [2, 768, 768], replicated, may hold values from -0.02734375 to 0.02734375
- w_key: bfloat16 [2, 768, 768], replicated, may hold values from -0.21875 to 0.21875
- w_value: bfloat16 [2, 768, 768], replicated, may hold values from -0.21875 to 0.21875
- w_output: bfloat16 [2, 768, 768], replicated, may hold values from -3.5 to 3.5
- rel_bias: float32 [32, 12], replicated, may hold values from -6 to 6
- gain_attn: float32 [2, 768], replicated, may hold values from 0.1 to 1.9
- gain_moe: float32 [2, 768], replicated, may hold values from 0.1 to 1.9
- w_router: float32 [2, 768, 4], replicated, may hold values from -0.21875 to 0.21875
- w_in: bfloat16 [2, 4, 768, 3072], P(None, 'expert'), may hold values from -0.21875 to 0.21875
- w_out: bfloat16 [2, 4, 3072, 768], P(None, 'expert'), may hold values from -0.3125 to 0.3125
- routes: int32 [2, 4, 1024, 1], P(None, 'dp', ('context', 'expert')), may hold values from 0 to 3; in each aligned block of 128 rows (0 to 127, 128 to 255, ..., all dimensions but the last counted through in order) at most 40 rows name the same one
- kept: int32 [2, 4, 1024], P(None, 'dp', ('context', 'expert')), may hold values 0 or 1
- cotangent: bfloat16 [4, 1024, 768], P('dp', ('context', 'expert')), may hold values from -6 to 6
Outputs:
- out: bfloat16 [4, 1024, 768], P('dp', ('context', 'expert'))
- d_tokens: float32 [4, 1024, 768], P('dp', ('context', 'expert'))
- grad_query: float32 [2, 768, 768], P(None, ('dp', 'context', 'expert'))
- grad_key: float32 [2, 768, 768], P(None, ('dp', 'context', 'expert'))
- grad_value: float32 [2, 768, 768], P(None, ('dp', 'context', 'expert'))
- grad_output: float32 [2, 768, 768], P(None, ('dp', 'context', 'expert'))
- grad_rel_bias: float32 [32, 12], replicated
- grad_gain_attn: float32 [2, 768], P(None, ('dp', 'context', 'expert'))
- grad_gain_moe: float32 [2, 768], P(None, ('dp', 'context', 'expert'))
- grad_router: float32 [2, 768, 4], P(None, ('dp', 'context', 'expert'))
- grad_in: float32 [2, 4, 768, 3072], P(None, 'expert', ('dp', 'context'))
- grad_out: float32 [2, 4, 3072, 768], P(None, 'expert', ('dp', 'context'))
Inputs may be any that keep to these rules, and one draw needn't show every extreme that they name: `routes`: in each layer, among the 128 positions of one sequence on one device (aligned groups), no expert is named more than 40 times, a bound that some block reaches. `kept`: 1 where a token is processed by its expert, 0 where it overflowed and passes on without the expert branch.
All inputs are finite; a program needn't handle non-finite values. No bound on the sum of `kept` on one device may be relied on, other than what follows from the above.
Results may differ from a plain program's by a relative error of at most 0.025.
Values may be sent and summed in bfloat16 or wider, within the bound.
A program may use at most 256 MiB of HBM per device.

v0:
```python
import jax
import jax.numpy as jnp
from jax import lax
from jax.sharding import PartitionSpec as P

highest = lax.Precision.HIGHEST
epsilon = 1e-06
thresholds = (12, 16, 23, 32, 46, 64, 91)


def passed_along(block, axis, distance):
    devices = range(lax.axis_size(axis))
    route = [((i - distance) % len(devices), i) for i in devices]
    return lax.ppermute(block, axis, route)


def root_norm(value, gain):
    return value * lax.rsqrt(jnp.mean(value * value, axis=-1, keepdims=True) + epsilon) * gain


def bucket_of(offset):
    distance = jnp.abs(offset)
    beyond = 8 + sum(((distance >= limit).astype(jnp.int32) for limit in thresholds))
    inside = jnp.where(distance < 8, distance, beyond)
    return inside + jnp.where(offset > 0, 16, 0)


def bucket_hot(first, width, buckets):
    offsets = first + lax.iota(jnp.int32, width)
    return (bucket_of(offsets)[:, None] == lax.iota(jnp.int32, buckets)[None, :]).astype(
        jnp.float32
    )


def spread_line(line, count):
    heads, width = line.shape
    tiled = jnp.tile(line, (1, count))[:, : count * (width - 1)]
    return tiled.reshape(heads, count, width - 1)[:, :, count - 1 :]


def fold_line(block, count, columns):
    heads = block.shape[0]
    width = count + columns
    padded = jnp.pad(block, ((0, 0), (0, 0), (count - 1, 0)))
    flat = jnp.pad(padded.reshape(heads, count * (width - 1)), ((0, 0), (0, count)))
    return jnp.sum(flat.reshape(heads, count, width), axis=1)


def split_product(form, weights, other):
    upper = weights.astype(jnp.bfloat16)
    lower = (weights - upper.astype(jnp.float32)).astype(jnp.bfloat16)
    return jnp.einsum(form, upper, other, preferred_element_type=jnp.float32) + jnp.einsum(
        form, lower, other, preferred_element_type=jnp.float32
    )


def block_scores(query, keys, table, first):
    batch, count, width = query.shape
    columns = keys.shape[1]
    heads = table.shape[1]
    onehot = bucket_hot(first, count + columns, table.shape[0])
    line = jnp.dot(onehot, table, precision=highest).T
    shaped_query = query.reshape(batch, count, heads, width // heads)
    shaped_keys = keys.reshape(batch, columns, heads, width // heads)
    scores = jnp.einsum(
        "sihd,sjhd->shij", shaped_query, shaped_keys, preferred_element_type=jnp.float32
    )
    return (scores + spread_line(line, count)[None], onehot)


def forward_block(state, pair, query, table, first):
    top, total, summed = state
    scores, unused = block_scores(query, pair[0], table, first)
    new_top = jnp.maximum(top, jnp.max(scores, axis=-1))
    factor = jnp.exp(top - new_top)
    weights = jnp.exp(scores - new_top[..., None])
    total = total * factor + jnp.sum(weights, axis=-1)
    batch, columns, width = pair.shape[1:]
    heads = top.shape[1]
    values = pair[1].reshape(batch, columns, heads, width // heads)
    summed = summed * factor[..., None] + split_product("shij,sjhd->shid", weights, values)
    return (new_top, total, summed)


def attend(query, pair, table, first_for, context_size):
    batch, count, width = query.shape
    heads = table.shape[1]
    start_state = (
        jnp.full((batch, heads, count), -1e30, jnp.float32),
        jnp.zeros((batch, heads, count), jnp.float32),
        jnp.zeros((batch, heads, count, width // heads), jnp.float32),
    )
    state = forward_block(start_state, pair, query, table, first_for(0))

    def step_fn(carry, step):
        moving, inner = carry
        moving = passed_along(moving, "context", 1)
        return ((moving, forward_block(inner, moving, query, table, first_for(step))), None)

    (unused, state), unused_out = lax.scan(
        step_fn, (pair, state), jnp.arange(1, context_size, dtype=jnp.int32)
    )
    top, total, summed = state
    merged = jnp.transpose(summed / total[..., None], (0, 2, 1, 3)).reshape(batch, count, width)
    return (merged, top + jnp.log(total))


def backward_block(query, grad_merged, delta, log_total, pair, table, first):
    scores, onehot = block_scores(query, pair[0], table, first)
    chances = jnp.exp(scores - log_total[..., None])
    batch, columns, width = pair.shape[1:]
    count = query.shape[1]
    heads = table.shape[1]
    keys = pair[0].reshape(batch, columns, heads, width // heads)
    values = pair[1].reshape(batch, columns, heads, width // heads)
    shaped_query = query.reshape(batch, count, heads, width // heads)
    shaped_grad = grad_merged.reshape(batch, count, heads, width // heads)
    dot_grad = jnp.einsum(
        "sihd,sjhd->shij", shaped_grad, values, preferred_element_type=jnp.float32
    )
    score_grad = (chances * (dot_grad - delta[..., None])).astype(jnp.bfloat16)
    query_grad = jnp.einsum("shij,sjhd->sihd", score_grad, keys, preferred_element_type=jnp.float32)
    key_grad = jnp.einsum(
        "shij,sihd->sjhd", score_grad, shaped_query, preferred_element_type=jnp.float32
    )
    value_grad = split_product("shij,sihd->sjhd", chances, shaped_grad)
    diagonal = fold_line(jnp.sum(score_grad.astype(jnp.float32), axis=0), count, columns)
    table_grad = jnp.einsum("wb,hw->bh", onehot, diagonal, precision=highest)
    pair_grad = jnp.stack(
        [key_grad.reshape(batch, columns, width), value_grad.reshape(batch, columns, width)]
    )
    return (query_grad.reshape(batch, count, width), pair_grad, table_grad)


def attend_back(
    query, grad_merged, delta, log_total, pair, table, first_for, source_for, context_size
):
    query_grad, pair_grad, table_grad = backward_block(
        query, grad_merged, delta, log_total, pair, table, first_for(0)
    )
    batch, columns, width = pair.shape[1:]
    steps = jnp.arange(1, context_size, dtype=jnp.int32)

    def move_keys(moving):
        return passed_along(moving, "context", 1)

    store = jnp.zeros((2, batch, context_size * columns, width), jnp.float32)
    store = lax.dynamic_update_slice_in_dim(store, pair_grad, source_for(0) * columns, 2)

    def step_fn(carry, step):
        moving, store_now, query_sum, table_sum = carry
        moving = move_keys(moving)
        more_query, more_pair, more_table = backward_block(
            query, grad_merged, delta, log_total, moving, table, first_for(step)
        )
        store_now = lax.dynamic_update_slice_in_dim(
            store_now, more_pair, source_for(step) * columns, 2
        )
        return ((moving, store_now, query_sum + more_query, table_sum + more_table), None)

    (unused, store, query_grad, table_grad), unused_out = lax.scan(
        step_fn, (pair, store, query_grad, table_grad), steps
    )
    own = lax.psum_scatter(
        store.astype(jnp.bfloat16), ("context", "expert"), scatter_dimension=2, tiled=True
    ).astype(jnp.float32)
    return (query_grad, own, table_grad)


def expert_apply(inner_w, outer_w, arrived):
    slots = arrived.shape[1]
    local = inner_w.shape[0]
    grouped = arrived.reshape(-1, local, slots, arrived.shape[2])
    before = jnp.einsum("gend,edf->genf", grouped, inner_w, preferred_element_type=jnp.float32)
    hidden = jax.nn.gelu(before).astype(jnp.bfloat16)
    answer = jnp.einsum(
        "genf,efd->gend", hidden, outer_w, preferred_element_type=jnp.float32
    ).astype(jnp.bfloat16)
    return (answer.reshape(arrived.shape), before.reshape(arrived.shape[0], slots, -1), arrived)


def on_device(
    tokens,
    w_query,
    w_key,
    w_value,
    w_output,
    rel_bias,
    gain_attn,
    gain_moe,
    w_router,
    w_in,
    w_out,
    routes,
    kept,
    cotangent,
):
    batch, count, width = tokens.shape
    layers = w_query.shape[0]
    heads = rel_bias.shape[1]
    experts = w_router.shape[2]
    local_experts = w_in.shape[1]
    hidden_width = w_in.shape[3]
    context_size = lax.axis_size("context")
    group = lax.axis_size("expert")
    here = lax.axis_index("context")
    place = lax.axis_index("expert")
    columns = group * count
    anchor = (here * group + place) * count
    token_count = batch * count
    room = count * 5 // (4 * experts)
    capacity = batch * room

    def source_for(step):
        return (here - step) % context_size

    def first_for(step):
        return source_for(step) * columns - anchor - (count - 1)

    residual = tokens.astype(jnp.float32).reshape(token_count, width)
    saved = []
    for layer in range(layers):
        normed_low = root_norm(residual, gain_attn[layer]).astype(jnp.bfloat16)
        query = (
            jnp.dot(normed_low, w_query[layer], preferred_element_type=jnp.float32)
            .astype(jnp.bfloat16)
            .reshape(batch, count, width)
        )
        keys = (
            jnp.dot(normed_low, w_key[layer], preferred_element_type=jnp.float32)
            .astype(jnp.bfloat16)
            .reshape(batch, count, width)
        )
        values = (
            jnp.dot(normed_low, w_value[layer], preferred_element_type=jnp.float32)
            .astype(jnp.bfloat16)
            .reshape(batch, count, width)
        )
        pair = lax.all_gather(jnp.stack([keys, values]), "expert", axis=2, tiled=True)
        merged, log_total = attend(query, pair, rel_bias, first_for, context_size)
        merged_low = merged.astype(jnp.bfloat16).reshape(token_count, width)
        middle = residual + jnp.dot(merged_low, w_output[layer], preferred_element_type=jnp.float32)
        moe_in = root_norm(middle, gain_moe[layer])
        router = jax.nn.softmax(jnp.dot(moe_in, w_router[layer], precision=highest), axis=-1)
        route = routes[layer][..., 0]
        chosen = (route[..., None] == lax.iota(jnp.int32, experts)).astype(jnp.int32)
        rank = jnp.sum(chosen * (jnp.cumsum(chosen, axis=1) - 1), axis=-1)
        target = route * capacity + lax.iota(jnp.int32, batch)[:, None] * room + rank
        live = kept[layer].reshape(token_count)
        select = (
            (lax.iota(jnp.int32, experts * capacity)[:, None] == target) & (live[None, :] > 0)
        ).astype(jnp.bfloat16)
        chosen_float = chosen.reshape(token_count, experts).astype(jnp.float32)
        live_float = live.astype(jnp.float32)
        gate = jnp.sum(router * chosen_float, axis=-1) * live_float
        sent = jnp.dot(
            select, moe_in.astype(jnp.bfloat16), preferred_element_type=jnp.float32
        ).astype(jnp.bfloat16)
        answer, before, arrived = expert_apply(
            w_in[layer],
            w_out[layer],
            lax.all_to_all(
                sent.reshape(experts, capacity, width),
                "expert",
                split_axis=0,
                concat_axis=0,
                tiled=True,
            ),
        )
        returned = lax.all_to_all(answer, "expert", split_axis=0, concat_axis=0, tiled=True)
        picked = jnp.einsum(
            "ct,cd->td",
            select,
            returned.reshape(experts * capacity, width),
            preferred_element_type=jnp.float32,
        )
        saved.append(
            (
                residual,
                normed_low,
                query,
                pair,
                merged,
                log_total,
                merged_low,
                middle,
                moe_in,
                router,
                chosen_float,
                live_float,
                gate,
                select,
                picked,
                before,
                arrived,
            )
        )
        residual = middle + gate[:, None] * picked
    output = residual.astype(jnp.bfloat16).reshape(batch, count, width)
    grad = cotangent.astype(jnp.float32).reshape(token_count, width)
    table_grad = jnp.zeros_like(rel_bias)
    query_list, key_list, value_list, output_list = ([], [], [], [])
    gain_attn_list, gain_moe_list, router_list, in_list, out_list = ([], [], [], [], [])
    for layer in reversed(range(layers)):
        (
            residual_in,
            normed_low,
            query,
            pair,
            merged,
            log_total,
            merged_low,
            middle,
            moe_in,
            router,
            chosen_float,
            live_float,
            gate,
            select,
            picked,
            before,
            arrived,
        ) = saved[layer]
        gate_grad = jnp.sum(grad * picked, axis=-1)
        answer_grad = (gate[:, None] * grad).astype(jnp.bfloat16)
        back_sent = jnp.dot(select, answer_grad, preferred_element_type=jnp.float32).astype(
            jnp.bfloat16
        )
        arrived_grad = lax.all_to_all(
            back_sent.reshape(experts, capacity, width),
            "expert",
            split_axis=0,
            concat_axis=0,
            tiled=True,
        )
        shaped_grad = arrived_grad.reshape(group, local_experts, capacity, width)
        shaped_in = arrived.reshape(group, local_experts, capacity, width)
        shaped_before = before.reshape(group, local_experts, capacity, hidden_width)
        hidden, slope = jax.vjp(jax.nn.gelu, shaped_before)
        hidden_low = hidden.astype(jnp.bfloat16)
        out_list.insert(
            0,
            jnp.einsum(
                "genf,gend->efd", hidden_low, shaped_grad, preferred_element_type=jnp.float32
            ),
        )
        hidden_grad = jnp.einsum(
            "gend,efd->genf", shaped_grad, w_out[layer], preferred_element_type=jnp.float32
        )
        before_grad = slope(hidden_grad)[0].astype(jnp.bfloat16)
        in_list.insert(
            0,
            jnp.einsum(
                "gend,genf->edf", shaped_in, before_grad, preferred_element_type=jnp.float32
            ),
        )
        arrived_back = jnp.einsum(
            "genf,edf->gend", before_grad, w_in[layer], preferred_element_type=jnp.float32
        ).astype(jnp.bfloat16)
        home_grad = lax.all_to_all(
            arrived_back.reshape(experts, capacity, width),
            "expert",
            split_axis=0,
            concat_axis=0,
            tiled=True,
        )
        moe_grad = jnp.einsum(
            "ct,cd->td",
            select,
            home_grad.reshape(experts * capacity, width),
            preferred_element_type=jnp.float32,
        )
        chance_grad = chosen_float * (gate_grad * live_float)[:, None]
        logit_grad = router * (chance_grad - jnp.sum(router * chance_grad, axis=-1, keepdims=True))
        router_list.insert(0, jnp.einsum("td,te->de", moe_in, logit_grad, precision=highest))
        moe_grad = moe_grad + jnp.einsum(
            "te,de->td", logit_grad, w_router[layer], precision=highest
        )
        unused, norm_back = jax.vjp(root_norm, middle, gain_moe[layer])
        middle_grad, moe_gain_grad = norm_back(moe_grad)
        gain_moe_list.insert(0, moe_gain_grad)
        grad = grad + middle_grad
        grad_low = grad.astype(jnp.bfloat16)
        output_list.insert(
            0, jnp.einsum("td,te->de", merged_low, grad_low, preferred_element_type=jnp.float32)
        )
        merged_grad = jnp.einsum(
            "te,de->td", grad_low, w_output[layer], preferred_element_type=jnp.float32
        ).astype(jnp.bfloat16)
        merged_grad = merged_grad.reshape(batch, count, width)
        delta = jnp.einsum(
            "sihd,sihd->shi",
            merged_grad.astype(jnp.float32).reshape(batch, count, heads, -1),
            merged.reshape(batch, count, heads, -1),
            precision=highest,
        )
        query_grad, pair_grad, more_table = attend_back(
            query,
            merged_grad,
            delta,
            log_total,
            pair,
            rel_bias,
            first_for,
            source_for,
            context_size,
        )
        table_grad = table_grad + more_table
        query_low = query_grad.astype(jnp.bfloat16).reshape(token_count, width)
        key_low = pair_grad[0].astype(jnp.bfloat16).reshape(token_count, width)
        value_low = pair_grad[1].astype(jnp.bfloat16).reshape(token_count, width)
        query_list.insert(
            0, jnp.einsum("td,te->de", normed_low, query_low, preferred_element_type=jnp.float32)
        )
        key_list.insert(
            0, jnp.einsum("td,te->de", normed_low, key_low, preferred_element_type=jnp.float32)
        )
        value_list.insert(
            0, jnp.einsum("td,te->de", normed_low, value_low, preferred_element_type=jnp.float32)
        )
        normed_grad = (
            jnp.einsum("te,de->td", query_low, w_query[layer], preferred_element_type=jnp.float32)
            + jnp.einsum("te,de->td", key_low, w_key[layer], preferred_element_type=jnp.float32)
            + jnp.einsum("te,de->td", value_low, w_value[layer], preferred_element_type=jnp.float32)
        )
        unused, norm_back = jax.vjp(root_norm, residual_in, gain_attn[layer])
        residual_grad, attn_gain_grad = norm_back(normed_grad)
        gain_attn_list.insert(0, attn_gain_grad)
        grad = grad + residual_grad
    query_out, key_out, value_out, output_out, gain_attn_out, gain_moe_out, router_out = (
        lax.psum_scatter(
            jnp.stack(query_list), ("dp", "context", "expert"), scatter_dimension=1, tiled=True
        ),
        lax.psum_scatter(
            jnp.stack(key_list), ("dp", "context", "expert"), scatter_dimension=1, tiled=True
        ),
        lax.psum_scatter(
            jnp.stack(value_list), ("dp", "context", "expert"), scatter_dimension=1, tiled=True
        ),
        lax.psum_scatter(
            jnp.stack(output_list), ("dp", "context", "expert"), scatter_dimension=1, tiled=True
        ),
        lax.psum_scatter(
            jnp.stack(gain_attn_list), ("dp", "context", "expert"), scatter_dimension=1, tiled=True
        ),
        lax.psum_scatter(
            jnp.stack(gain_moe_list), ("dp", "context", "expert"), scatter_dimension=1, tiled=True
        ),
        lax.psum_scatter(
            jnp.stack(router_list), ("dp", "context", "expert"), scatter_dimension=1, tiled=True
        ),
    )
    in_out, out_out = (
        lax.psum_scatter(
            jnp.stack(in_list).astype(jnp.bfloat16),
            ("dp", "context"),
            scatter_dimension=2,
            tiled=True,
        ).astype(jnp.float32),
        lax.psum_scatter(
            jnp.stack(out_list).astype(jnp.bfloat16),
            ("dp", "context"),
            scatter_dimension=2,
            tiled=True,
        ).astype(jnp.float32),
    )
    bias_out = lax.psum(table_grad, ("dp", "context", "expert"))
    return (
        output,
        grad.reshape(batch, count, width),
        query_out,
        key_out,
        value_out,
        output_out,
        bias_out,
        gain_attn_out,
        gain_moe_out,
        router_out,
        in_out,
        out_out,
    )


def solution(mesh):
    in_specs = (
        P("dp", ("context", "expert"), None),
        P(),
        P(),
        P(),
        P(),
        P(),
        P(),
        P(),
        P(),
        P(None, "expert", None, None),
        P(None, "expert", None, None),
        P(None, "dp", ("context", "expert"), None),
        P(None, "dp", ("context", "expert")),
        P("dp", ("context", "expert"), None),
    )
    out_specs = (
        P("dp", ("context", "expert"), None),
        P("dp", ("context", "expert"), None),
        P(None, ("dp", "context", "expert"), None),
        P(None, ("dp", "context", "expert"), None),
        P(None, ("dp", "context", "expert"), None),
        P(None, ("dp", "context", "expert"), None),
        P(),
        P(None, ("dp", "context", "expert")),
        P(None, ("dp", "context", "expert")),
        P(None, ("dp", "context", "expert"), None),
        P(None, "expert", ("dp", "context"), None),
        P(None, "expert", ("dp", "context"), None),
    )
    return jax.shard_map(
        on_device, mesh=mesh, in_specs=in_specs, out_specs=out_specs, check_vma=False
    )
```

profile of v0, /device:TPU:0, one launch (start us, length us, event | category | flops | bytes accessed | tf_op | source)
XLA Modules:
  0.0 1240.6 jit_solution(14174580944938086444)
XLA Ops:
  20.3 7.6 reshape.1375
  35.3 7.0 reshape.1378
  42.6 10.8 all-gather.3.cloned.1.call-done
  64.6 25.1 %collective-permute-done = bf16[2,1,512,768]{3,2,1,0:T(8,128)(2,1)} collective-permute-done((bf16[2,1,512,768]{3,2,1,0:T(8,128)(2,1)}, bf16[2,1,512,768]{3,2,1,0:T(8,128)(2,1)}, u32[]{:S(2)}, u32[]{:S(2)}) %collective-permute-start) | collective-permute-done | bytes 1572896 | tf_op jit(solution)/shard_map/while/body/eval_jaxpr/ppermute | solution.py:14
  115.0 5.6 all-to-all-done
  146.3 35.9 %all-gather.5.cloned.1.call-done = bf16[2,1,512,768]{3,2,1,0:T(8,128)(2,1)} async-done(((bf16[2,1,128,768]{3,2,1,0:T(8,128)(2,1)}), bf16[2,1,512,768]{3,2,1,0:T(8,128)(2,1)}) %all-gather.5.cloned.1.call-update) | async-done | bytes 1572880 | tf_op jit(solution)/shard_map/all_gather | solution.py:239
  195.1 5.8 fusion.400
  200.9 17.6 %collective-permute-done.1 = bf16[2,1,512,768]{3,2,1,0:T(8,128)(2,1)} collective-permute-done((bf16[2,1,512,768]{3,2,1,0:T(8,128)(2,1)}, bf16[2,1,512,768]{3,2,1,0:T(8,128)(2,1)}, u32[]{:S(2)}, u32[]{:S(2)}) %collective-permute-start.1) | collective-permute-done | bytes 1572896 | tf_op jit(solution)/shard_map/while/body/eval_jaxpr/ppermute | solution.py:14
  223.5 5.5 fusion.401
  245.1 10.2 all_to_all.40
  280.2 10.2 all_to_all.41
  290.3 5.2 fusion.89
  296.5 4.7 fusion.143
  336.6 15.8 %copy.106 = bf16[2,1,1024,768]{3,1,0,2:T(2,128)(2,1)} copy(bf16[2,1,1024,768]{2,3,1,0:T(8,128)(2,1)} %maximum_dynamic-update-slice_fusion.1) | data formatting | bytes 6291456
  352.4 22.3 %bitcast_reduce_fusion.1 = bf16[1024,2,768]{2,1,0:T(2,128)(2,1)S(1)} fusion(bf16[2,1,1024,768]{3,1,0,2:T(2,128)(2,1)} %copy.106), kind=kLoop, calls=%fused_computation.7 | loop fusion | bytes 6291456
  382.1 69.3 %reduce-scatter.28.cloned.1.call-done = bf16[128,1536]{1,0:T(8,128)(2,1)} async-done(((bf16[1024,1536]{1,0:T(8,128)(2,1)}), bf16[128,1536]{1,0:T(8,128)(2,1)}) %reduce-scatter.28.cloned.1.call-update) | async-done | bytes 393232
  464.7 10.7 all_to_all.42
  475.4 4.7 fusion.84
  511.9 11.5 copy.108
  523.4 22.3 %bitcast_reduce_fusion = bf16[1024,2,768]{2,1,0:T(2,128)(2,1)S(1)} fusion(bf16[2,1,1024,768]{3,1,0,2:T(2,128)(2,1)} %copy.108), kind=kLoop, calls=%fused_computation.6 | loop fusion | bytes 6291456
  557.5 8.4 pad_maximum_fusion
  566.8 5.6 fusion.19
  576.4 8.3 pad_maximum_fusion.1
  592.3 6.7 reshape.1413
  641.1 5.7 reshape.1419
  646.8 6.5 reshape.1422
  682.2 41.5 %all-reduce.11 = (f32[32,12]{0,1:T(8,128)}, f32[2,768]{1,0:T(2,128)S(1)}, f32[2,768]{1,0:T(2,128)S(1)}, f32[2,768,4]{1,2,0:T(4,128)S(1)}) all-reduce(f32[32,12]{0,1:T(8,128)S(1)} %fusion.216, f32[2,768]{1,0:T(2,128)S(1)} %pad_maximum_fusion.9, ...), channel_id=1, replica_groups=mesh['dp'=4,'context'=2,'expert'=4] {'dp','context','expert'}, use_global_device_ids=true, to_apply=%region_40.41 | all-reduce | flops 9600 | bytes 76800 | tf_op jit(solution)/shard_map/psum | solution.py:467
  729.5 52.8 %reduce-scatter.26.cloned.1.call-done = bf16[2,1,384,768]{3,2,1,0:T(8,128)(2,1)} async-done(((bf16[2,1,3072,768]{3,2,1,0:T(8,128)(2,1)}), bf16[2,1,384,768]{3,2,1,0:T(8,128)(2,1)}) %reduce-scatter.26.cloned.1.call-update) | async-done | bytes 1179664 | tf_op jit(solution)/shard_map/reduce_scatter | solution.py:460
  785.2 110.2 %reduce-scatter.16.cloned.1.call-done = f32[2,24,768]{2,1,0:T(8,128)} async-done(((f32[2,768,768]{2,1,0:T(8,128)}), f32[2,24,768]{2,1,0:T(8,128)}) %reduce-scatter.16.cloned.1.call-update) | async-done | bytes 147472 | tf_op jit(solution)/shard_map/reduce_scatter | solution.py:431
  895.4 113.1 %reduce-scatter.22.cloned.1.call-done = f32[2,24,768]{2,1,0:T(8,128)} async-done(((f32[2,768,768]{2,1,0:T(8,128)}), f32[2,24,768]{2,1,0:T(8,128)}) %reduce-scatter.22.cloned.1.call-update) | async-done | bytes 147472 | tf_op jit(solution)/shard_map/reduce_scatter | solution.py:440
  1008.5 112.2 %reduce-scatter.18.cloned.1.call-done = f32[2,24,768]{2,1,0:T(8,128)} async-done(((f32[2,768,768]{2,1,0:T(8,128)}), f32[2,24,768]{2,1,0:T(8,128)}) %reduce-scatter.18.cloned.1.call-update) | async-done | bytes 147472 | tf_op jit(solution)/shard_map/reduce_scatter | solution.py:434
  1120.7 112.9 %reduce-scatter.20.cloned.1.call-done = f32[2,24,768]{2,1,0:T(8,128)} async-done(((f32[2,768,768]{2,1,0:T(8,128)}), f32[2,24,768]{2,1,0:T(8,128)}) %reduce-scatter.20.cloned.1.call-update) | async-done | bytes 147472 | tf_op jit(solution)/shard_map/reduce_scatter | solution.py:437
  (565 shorter events, 332.5 us)
Async XLA Ops:
  7.2 46.2 %all-gather.3.cloned.1.call-start = ((), (), s32[]{:S(2)}) async-start(), calls=%async_computation.16 | async-start | bytes 1966080 | tf_op jit(solution)/shard_map/all_gather | solution.py:239
  8.0 19.9 %copy-start.87 = (f32[768]{0:T(1024)}, f32[768]{0:T(1024)S(1)}, u32[]{:S(2)}) copy-start(f32[768]{0:T(1024)S(1)} %get-tuple-element.125) | copy-start | bytes 9220
  8.0 134.6 %copy-start.91 = (f32[768]{0:T(1024)}, f32[768]{0:T(1024)S(1)}, u32[]{:S(2)}) copy-start(f32[768]{0:T(1024)S(1)} %get-tuple-element.124) | copy-start | bytes 9220
  9.1 18.8 %copy-start.118 = (f32[128]{0:T(128)}, f32[128]{0:T(128)S(1)}, u32[]{:S(2)}) copy-start(f32[128]{0:T(128)S(1)} %fusion.377) | copy-start | bytes 1540
  28.4 68.5 %copy-start.52 = (bf16[128,768]{0,1:T(8,128)(2,1)}, bf16[128,768]{0,1:T(8,128)(2,1)S(1)}, u32[]{:S(2)}) copy-start(bf16[128,768]{0,1:T(8,128)(2,1)S(1)} %copy.78) | copy-start | bytes 589828
  35.3 19.9 %copy-start.121 = (f32[2,768]{1,0:T(2,128)S(1)}, f32[2,768]{1,0:T(2,128)}, u32[]{:S(2)}) copy-start(f32[2,768]{1,0:T(2,128)} %param.21) | copy-start | bytes 18436
  35.3 20.6 %copy-start.141 = (s32[2,1,128]{2,1,0:T(1,128)S(1)}, s32[2,1,128]{2,1,0:T(1,128)}, u32[]{:S(2)}) copy-start(s32[2,1,128]{2,1,0:T(1,128)} %param.26) | copy-start | bytes 3076
  53.4 36.3 %collective-permute-start = (bf16[2,1,512,768]{3,2,1,0:T(8,128)(2,1)}, bf16[2,1,512,768]{3,2,1,0:T(8,128)(2,1)}, u32[]{:S(2)}, u32[]{:S(2)}) collective-permute-start(bf16[2,1,512,768]{3,2,1,0:T(8,128)(2,1)} %all-gather.3.cloned.1.call-done), channel_id=1, source_target_pairs={{4,0},{0,4},{5,1},{1,5},{6,2},{2,6},{7,3},{3,7},{12,8},{8,12},{13,... | collective-permute-start | bytes 4718600 | tf_op jit(solution)/shard_map/while/body/eval_jaxpr/ppermute | solution.py:14
  55.7 56.8 %copy-start.81 = (f32[768]{0:T(1024)}, f32[768]{0:T(1024)S(1)}, u32[]{:S(2)}) copy-start(f32[768]{0:T(1024)S(1)} %get-tuple-element.123) | copy-start | bytes 9220
  108.5 12.1 all-to-all-start
  129.7 10.7 all-to-all-start.1
  133.8 48.5 %all-gather.5.cloned.1.call-start = ((), (), s32[]{:S(2)}) async-start(), calls=%async_computation.17 | async-start | bytes 1966080 | tf_op jit(solution)/shard_map/all_gather | solution.py:239
  182.3 36.3 %collective-permute-start.1 = (bf16[2,1,512,768]{3,2,1,0:T(8,128)(2,1)}, bf16[2,1,512,768]{3,2,1,0:T(8,128)(2,1)}, u32[]{:S(2)}, u32[]{:S(2)}) collective-permute-start(bf16[2,1,512,768]{3,2,1,0:T(8,128)(2,1)} %all-gather.5.cloned.1.call-done), channel_id=1, source_target_pairs={{4,0},{0,4},{5,1},{1,5},{6,2},{2,6},{7,3},{3,7},{12,8},{8,12},{13,... | collective-permute-start | bytes 4718600 | tf_op jit(solution)/shard_map/while/body/eval_jaxpr/ppermute | solution.py:14
  240.7 20.1 %slice-start.2 = ((s8[9437184]{0:T(1024)(128)(4,1)}), s8[1048576]{0:T(1024)(128)(4,1)S(1)}, s32[]{:S(2)}) async-start(s8[9437184]{0:T(1024)(128)(4,1)} %bitcast.722), calls=%async_computation.28 | async-start | bytes 2097152
  241.8 18.9 %slice-start.3 = ((s8[9437184]{0:T(1024)(128)(4,1)}), s8[4194304]{0:T(1024)(128)(4,1)S(1)}, s32[]{:S(2)}) async-start(s8[9437184]{0:T(1024)(128)(4,1)} %bitcast.722), calls=%async_computation.29 | async-start | bytes 8388608
  262.8 10.9 all-to-all-start.3
  301.2 10.7 all-to-all-start.5
  305.2 146.2 %reduce-scatter.28.cloned.1.call-start = ((), (), s32[]{:S(2)}) async-start(), calls=%async_computation.24 | async-start | bytes 3538944
  382.1 77.9 %copy-start.92 = (f32[768]{0:T(1024)S(1)}, f32[768]{0:T(1024)}, u32[]{:S(2)}) copy-start(f32[768]{0:T(1024)} %copy-done.91) | copy-start | bytes 9220
  382.1 77.9 %copy-start.130 = (f32[128]{0:T(128)S(1)}, f32[128]{0:T(128)}, u32[]{:S(2)}) copy-start(f32[128]{0:T(128)} %copy-done.129) | copy-start | bytes 1540
  460.1 21.0 %slice-start.5 = ((s8[9437184]{0:T(1024)(128)(4,1)}), s8[4194304]{0:T(1024)(128)(4,1)S(1)}, s32[]{:S(2)}) async-start(s8[9437184]{0:T(1024)(128)(4,1)} %bitcast.724), calls=%async_computation.31 | async-start | bytes 8388608
  483.5 10.7 all-to-all-start.7
  487.5 165.8 %reduce-scatter.30.cloned.1.call-start = ((), (), s32[]{:S(2)}) async-start(), calls=%async_computation.25 | async-start | bytes 3538944
  548.1 178.4 %reduce-scatter.24.cloned.1.call-start = ((), (), s32[]{:S(2)}) async-start(), calls=%async_computation.22 | async-start | bytes 10616832 | tf_op jit(solution)/shard_map/reduce_scatter | solution.py:454
  565.9 216.4 %reduce-scatter.26.cloned.1.call-start = ((), (), s32[]{:S(2)}) async-start(), calls=%async_computation.23 | async-start | bytes 10616832 | tf_op jit(solution)/shard_map/reduce_scatter | solution.py:460
  584.8 310.6 %reduce-scatter.16.cloned.1.call-start = ((), (), s32[]{:S(2)}) async-start(), calls=%async_computation.18 | async-start | bytes 4866048 | tf_op jit(solution)/shard_map/reduce_scatter | solution.py:431
  613.5 395.0 %reduce-scatter.22.cloned.1.call-start = ((), (), s32[]{:S(2)}) async-start(), calls=%async_computation.21 | async-start | bytes 4866048 | tf_op jit(solution)/shard_map/reduce_scatter | solution.py:440
  622.1 498.6 %reduce-scatter.18.cloned.1.call-start = ((), (), s32[]{:S(2)}) async-start(), calls=%async_computation.19 | async-start | bytes 4866048 | tf_op jit(solution)/shard_map/reduce_scatter | solution.py:434
  665.0 568.6 %reduce-scatter.20.cloned.1.call-start = ((), (), s32[]{:S(2)}) async-start(), calls=%async_computation.20 | async-start | bytes 4866048 | tf_op jit(solution)/shard_map/reduce_scatter | solution.py:437
  680.6 45.0 %copy-start.143 = (f32[128]{0:T(128)S(1)}, f32[128]{0:T(128)}, u32[]{:S(2)}) copy-start(f32[128]{0:T(128)} %copy-done.142) | copy-start | bytes 1540
  680.6 45.1 %copy-start.48 = (f32[128,768]{1,0:T(8,128)S(1)}, f32[128,768]{1,0:T(8,128)}, u32[]{:S(2)}) copy-start(f32[128,768]{1,0:T(8,128)} %copy-done.46) | copy-start | bytes 1179652
  726.6 507.0 %copy-start.1 = (f32[32,12]{0,1:T(8,128)S(1)}, f32[32,12]{0,1:T(8,128)}, u32[]{:S(2)}) copy-start(f32[32,12]{0,1:T(8,128)} %param.19) | copy-start | bytes 4612
  (150 other events, 504.1 us)
Sparse Core Ops, SparseCore 0:
  13.6 39.7 all-gather.2
  146.4 35.7 all-gather.4
  377.1 74.2 reduce-scatter.27
  548.2 74.4 reduce-scatter.29
  626.1 76.3 reduce-scatter.23
  705.9 76.4 reduce-scatter.25
  788.4 106.9 reduce-scatter.15
  902.4 106.0 reduce-scatter.21
  1014.5 106.0 reduce-scatter.17
  1127.5 106.0 reduce-scatter.19
where the time goes:
time: 1250 us; the launch traced here: 1240 us
  waiting for transfers between devices  682 us (55%)
  local copies, waits for them, and re-layouts  219 us (18%)
  matrix products  151 us (12%)
  other arithmetic  75.6 us (6%)
  blocking collectives  72.5 us (6%)
  starting transfers between devices  24.8 us (2%)
  between operations  16.4 us (1%)
    unnamed x352, local copies, waits for them, and re-layouts  127 us
    reduce_scatter x1, waiting for transfers between devices, on_device(): lax.psum_scatter(jnp.stack(output_list), ('dp', 'context', 'expert'), sca...  113 us
    reduce_scatter x1, waiting for transfers between devices, on_device(): lax.psum_scatter(jnp.stack(value_list), ('dp', 'context', 'expert'), scat...  113 us
    reduce_scatter x1, waiting for transfers between devices, on_device(): lax.psum_scatter(jnp.stack(key_list), ('dp', 'context', 'expert'), scatte...  112 us
    reduce_scatter x1, waiting for transfers between devices, on_device(): lax.psum_scatter(jnp.stack(query_list), ('dp', 'context', 'expert'), scat...  110 us
    unnamed x12, waiting for transfers between devices  69.5 us
    reduce_scatter x1, waiting for transfers between devices, on_device(): lax.psum_scatter(jnp.stack(out_list).astype(jnp.bfloat16), ('dp', 'contex...  52.8 us
    all_gather x2, waiting for transfers between devices, on_device(): lax.all_gather(jnp.stack([keys, values]), 'expert', axis=2, tiled=True)  46.8 us
  transfers between devices with their start and end apart: 17, of which 15 were waited for; matrix products, arithmetic and copies ran while one was open for 16% of the time, Pallas kernels for 0%

commit v1 on v0

--- a/solution.py
+++ b/solution.py
@@ -1,11 +1,480 @@
+import functools
+
 import jax
 import jax.numpy as jnp
+import numpy as np
 from jax import lax
+from jax.experimental import pallas as pl
+from jax.experimental.pallas import tpu as pltpu
 from jax.sharding import PartitionSpec as P
 
 highest = lax.Precision.HIGHEST
 epsilon = 1e-06
 thresholds = (12, 16, 23, 32, 46, 64, 91)
+MESH = pl.DeviceIdType.MESH
+GROUP = 4
+HEAD = 64
+BLOCK = 128
+FCHUNK = 512
+f32, bf16 = jnp.float32, jnp.bfloat16
+
+
+def div(a, b):
+    return lax.div(a, jnp.int32(b))
+
+
+def rem(a, b):
+    return lax.rem(a, jnp.int32(b))
+
+
+class Place:
+    def __init__(self, parts, experts):
+        self.parts, self.experts = parts, experts
+        self.dp = lax.axis_index("dp")
+        self.context = lax.axis_index("context")
+        self.expert = lax.axis_index("expert")
+        self.core = rem(self.dp, 2)
+        self.far = div(self.context, 2)
+        self.block = 2 * rem(self.context, 2) + div(self.dp, 2)
+        self.part = 2 * self.far + self.core
+
+    def flipped(self, flip):
+        low = rem(rem(self.block, 2) + flip % 2, 2)
+        high = rem(div(self.block, 2) + flip // 2, 2)
+        return 2 * high + low
+
+    def group_device(self, block):
+        return {"dp": 2 * rem(block, 2) + self.core, "context": 2 * self.far + div(block, 2)}
+
+    def part_other(self, step):
+        return rem(self.part + step, self.parts)
+
+    def part_device(self, part):
+        return {
+            "dp": self.dp - self.core + rem(part, 2),
+            "context": 2 * div(part, 2) + rem(self.context, 2),
+        }
+
+    def expert_other(self, step):
+        return rem(self.expert + step, self.experts)
+
+    def offset(self, part, block, query_block):
+        return 8 * (part // 2 - self.far) + 2 * (block - query_block) + (part % 2 - self.core)
+
+    def bias_index(self, part, block, query_block):
+        offset = self.offset(part, block, query_block)
+        return jnp.minimum(jnp.maximum(offset, -2), 2) + 2
+
+    def greet(self, expert=True):
+        partners = [self.group_device(self.flipped(flip)) for flip in (1, 2, 3)]
+        partners += [self.part_device(self.part_other(step)) for step in range(1, self.parts)]
+        if expert:
+            partners += [{"expert": self.expert_other(step)} for step in range(1, self.experts)]
+        barrier = pltpu.get_barrier_semaphore()
+        for partner in partners:
+            pl.semaphore_signal(barrier, inc=1, device_id=partner, device_id_type=MESH)
+        pl.semaphore_wait(barrier, len(partners))
+
+
+def remote(source, target, send, receive, device):
+    return pltpu.make_async_remote_copy(
+        src_ref=source,
+        dst_ref=target,
+        send_sem=send,
+        recv_sem=receive,
+        device_id=device,
+        device_id_type=MESH,
+    )
+
+
+def dot(a, b):
+    return jnp.dot(a, b, preferred_element_type=f32)
+
+
+def dot_nt(a, b):
+    return lax.dot_general(a, b, (((1,), (1,)), ((), ())), preferred_element_type=f32)
+
+
+def dot_tn(a, b):
+    return lax.dot_general(a, b, (((0,), (0,)), ((), ())), preferred_element_type=f32)
+
+
+def root_scale(value):
+    return lax.rsqrt(jnp.mean(value * value, axis=-1, keepdims=True) + epsilon)
+
+
+def lanes(rows, width):
+    return lax.broadcasted_iota(jnp.int32, (rows, width), 1)
+
+
+def gelu_parts(value):
+    scale = 0.7978845608028654
+    square = value * value
+    inner = jnp.tanh(scale * (value + 0.044715 * (square * value)))
+    half = 0.5 * (1.0 + inner)
+    slope = half + 0.5 * value * (1.0 - inner * inner) * (scale * (1.0 + 3 * 0.044715 * square))
+    return value * half, slope
+
+
+def gelu(value):
+    scale = 0.7978845608028654
+    return value * (0.5 * (1.0 + jnp.tanh(scale * (value + 0.044715 * (value * value * value)))))
+
+
+def forward_kernel(
+    layer,
+    parts,
+    experts,
+    x,
+    gains,
+    w_router,
+    select,
+    chosen,
+    bias,
+    w_qkv_hbm,
+    w_output_hbm,
+    w_in_hbm,
+    w_out_hbm,
+    normed,
+    query,
+    pair,
+    merged,
+    log_total,
+    merged_low,
+    middle,
+    router,
+    picked,
+    arrived,
+    before,
+    x_next,
+    w_qkv,
+    w_output,
+    w_in,
+    w_out,
+    scores,
+    merged_mine,
+    slots,
+    total,
+    answer,
+    returned,
+    load_sem,
+    group_send,
+    group_recv,
+    part_send,
+    part_recv,
+    merge_send,
+    merge_recv,
+    slot_send,
+    slot_recv,
+    back_send,
+    back_recv,
+):
+    here = Place(parts, experts)
+    heads = 3
+    wide = heads * HEAD
+    loads = [
+        pltpu.make_async_copy(w_qkv_hbm.at[layer], w_qkv, load_sem.at[0]),
+        pltpu.make_async_copy(w_output_hbm.at[layer], w_output, load_sem.at[1]),
+        pltpu.make_async_copy(w_in_hbm.at[layer, 0], w_in, load_sem.at[2]),
+        pltpu.make_async_copy(w_out_hbm.at[layer, 0], w_out, load_sem.at[3]),
+    ]
+    for load in loads:
+        load.start()
+    value = x[...]
+    block = here.block
+    normed[block] = (value * root_scale(value) * gains[0:1, :]).astype(bf16)
+    here.greet()
+
+    def gather(flip, source):
+        return remote(
+            normed.at[source],
+            normed.at[source],
+            group_send.at[flip - 1],
+            group_recv.at[flip - 1],
+            here.group_device(here.flipped(flip)),
+        )
+
+    for flip in (1, 2, 3):
+        gather(flip, block).start()
+
+    def hand_pair(step, part, of_block):
+        return remote(
+            pair.at[part, of_block],
+            pair.at[part, of_block],
+            part_send.at[step - 1, of_block],
+            part_recv.at[step - 1, of_block],
+            here.part_device(here.part_other(step)),
+        )
+
+    def project(of_block):
+        made = dot(normed[of_block], w_qkv[...]).astype(bf16)
+        pair[here.part, of_block] = made[:, : 2 * wide]
+        query[of_block] = made[:, 2 * wide :]
+        for step in range(1, parts):
+            hand_pair(step, here.part, of_block).start()
+
+    loads[0].wait()
+    project(block)
+    for flip in (1, 2, 3):
+        source = here.flipped(flip)
+        gather(flip, source).wait_recv()
+        project(source)
+    for step in range(1, parts):
+        source = rem(here.part + parts - step, parts)
+        for of_block in range(GROUP):
+            hand_pair(step, source, of_block).wait_recv()
+
+    lane = lanes(BLOCK, wide)
+    lane_out = lanes(BLOCK, 2 * BLOCK)
+    lane_log = lanes(BLOCK, BLOCK)
+
+    def hand_merged(flip, source):
+        return remote(
+            merged_mine.at[here.flipped(flip)],
+            merged_low.at[source],
+            merge_send.at[flip - 1],
+            merge_recv.at[flip - 1],
+            here.group_device(here.flipped(flip)),
+        )
+
+    for flip in (3, 1, 2, 0):
+        mine = here.flipped(flip)
+        rows = query[mine]
+        gathered = jnp.zeros((BLOCK, 2 * BLOCK), f32)
+        logs = jnp.zeros((BLOCK, BLOCK), f32)
+        for head in range(heads):
+            masked = jnp.where(lane // HEAD == head, rows, jnp.zeros_like(rows))
+            top = jnp.full((BLOCK, 1), -1e30, f32)
+            for part in range(parts):
+                keys = pair[part].reshape(GROUP * BLOCK, 2 * wide)[:, :wide]
+                raw = dot_nt(masked, keys)
+                for of_block in range(GROUP):
+                    piece = (
+                        raw[:, of_block * BLOCK : (of_block + 1) * BLOCK]
+                        + bias[head, here.bias_index(part, of_block, mine)]
+                    )
+                    scores[part * GROUP + of_block] = piece
+                    top = jnp.maximum(top, jnp.max(piece, axis=-1, keepdims=True))
+            summed = jnp.zeros((BLOCK, 1), f32)
+            out = jnp.zeros((BLOCK, 2 * BLOCK), f32)
+            for part in range(parts):
+                pieces = []
+                for of_block in range(GROUP):
+                    weight = jnp.exp(scores[part * GROUP + of_block] - top)
+                    summed = summed + jnp.sum(weight, axis=-1, keepdims=True)
+                    pieces.append(weight.astype(bf16))
+                values = pair[part].reshape(GROUP * BLOCK, 2 * wide)[:, BLOCK:]
+                out = out + dot(jnp.concatenate(pieces, axis=1), values)
+            gathered = jnp.where((lane_out + HEAD) // HEAD == head + 2, out / summed, gathered)
+            logs = jnp.where(lane_log == head, top + jnp.log(summed), logs)
+        final = gathered[:, HEAD:]
+        merged[mine] = final
+        log_total[mine] = logs
+        if flip:
+            merged_mine[mine] = final.astype(bf16)
+            hand_merged(flip, block).start()
+        else:
+            merged_low[block] = final.astype(bf16)
+
+    for flip in (1, 2, 3):
+        hand_merged(flip, here.flipped(flip)).wait_recv()
+    loads[1].wait()
+    mid = value
+    for of_block in range(GROUP):
+        mid = mid + dot(merged_low[of_block], w_output[of_block * wide : (of_block + 1) * wide, :])
+    middle[...] = mid
+    moe_in = mid * root_scale(mid) * gains[1:2, :]
+    moe_low = moe_in.astype(bf16)
+
+    def hand_slots(step, source):
+        return remote(
+            slots.at[here.expert_other(step)],
+            arrived.at[source],
+            slot_send.at[step - 1],
+            slot_recv.at[step - 1],
+            {"expert": here.expert_other(step)},
+        )
+
+    for expert in range(experts):
+        slots[expert] = dot(select[expert], moe_low).astype(bf16)
+    for step in range(1, experts):
+        hand_slots(step, here.expert).start()
+    arrived[here.expert] = slots[here.expert]
+    logits = jnp.dot(moe_in, w_router[...], precision=highest, preferred_element_type=f32)
+    logits = jnp.where(lane_log < experts, logits, -1e30)
+    raised = jnp.exp(logits - jnp.max(logits, axis=-1, keepdims=True))
+    chances = raised / jnp.sum(raised, axis=-1, keepdims=True)
+    router[...] = chances
+    gate = jnp.sum(chances * chosen[...], axis=-1, keepdims=True)
+    loads[2].wait()
+    loads[3].wait()
+    for step in range(1, experts):
+        hand_slots(step, rem(here.expert + experts - step, experts)).wait_recv()
+    given = jnp.concatenate([arrived[expert].astype(f32) for expert in range(experts)], axis=0)
+    given = given.astype(bf16)
+    room = arrived.shape[1]
+    total[...] = jnp.zeros_like(total)
+
+    @pl.loop(0, w_in.shape[1] // FCHUNK)
+    def _(index):
+        columns = pl.ds(pl.multiple_of(index * FCHUNK, FCHUNK), FCHUNK)
+        first = dot(given, w_in[:, columns])
+        before[:, columns] = first
+        total[...] += dot(gelu(first).astype(bf16), w_out[columns, :])
+
+    def hand_answer(step, source):
+        return remote(
+            answer.at[here.expert_other(step)],
+            returned.at[source],
+            back_send.at[step - 1],
+            back_recv.at[step - 1],
+            {"expert": here.expert_other(step)},
+        )
+
+    for expert in range(experts):
+        answer[expert] = total[expert * room : (expert + 1) * room, :].astype(bf16)
+    for step in range(1, experts):
+        hand_answer(step, here.expert).start()
+    returned[here.expert] = answer[here.expert]
+    for step in range(1, experts):
+        hand_answer(step, rem(here.expert + experts - step, experts)).wait_recv()
+    back = jnp.zeros_like(value)
+    for expert in range(experts):
+        back = back + dot_tn(select[expert], returned[expert])
+    picked[...] = back.astype(bf16)
+    x_next[...] = mid + gate * back
+    for flip in (1, 2, 3):
+        gather(flip, block).wait_send()
+        hand_merged(flip, block).wait_send()
+    for step in range(1, parts):
+        for of_block in range(GROUP):
+            hand_pair(step, here.part, of_block).wait_send()
+    for step in range(1, experts):
+        hand_slots(step, here.expert).wait_send()
+        hand_answer(step, here.expert).wait_send()
+
+
+VMEM = pl.BlockSpec(memory_space=pltpu.VMEM)
+ANY = pl.BlockSpec(memory_space=pl.ANY)
+DMA = pltpu.SemaphoreType.DMA
+
+
+def forward_layer(layer, x, gains, w_router, select, chosen, bias, w_qkv, w_output, w_in, w_out):
+    count, width = x.shape
+    parts, experts = lax.axis_size("context"), lax.axis_size("expert")
+    wide = w_qkv.shape[2] // 3
+    room = select.shape[1]
+    hidden = w_in.shape[3]
+    shape = jax.ShapeDtypeStruct
+    return pl.pallas_call(
+        functools.partial(forward_kernel, layer, parts, experts),
+        out_shape=[
+            shape((GROUP, count, width), bf16),
+            shape((GROUP, count, wide), bf16),
+            shape((parts, GROUP, count, 2 * wide), bf16),
+            shape((GROUP, count, wide), f32),
+            shape((GROUP, count, 128), f32),
+            shape((GROUP, count, wide), bf16),
+            shape((count, width), f32),
+            shape((count, 128), f32),
+            shape((count, width), bf16),
+            shape((experts, room, width), bf16),
+            shape((experts * room, hidden), f32),
+            shape((count, width), f32),
+        ],
+        in_specs=[VMEM] * 6 + [ANY] * 4,
+        out_specs=[VMEM] * 12,
+        scratch_shapes=[
+            pltpu.VMEM((width, 3 * wide), bf16),
+            pltpu.VMEM((width, width), bf16),
+            pltpu.VMEM((width, hidden), bf16),
+            pltpu.VMEM((hidden, width), bf16),
+            pltpu.VMEM((parts * GROUP, count, BLOCK), f32),
+            pltpu.VMEM((GROUP, count, wide), bf16),
+            pltpu.VMEM((experts, room, width), bf16),
+            pltpu.VMEM((experts * room, width), f32),
+            pltpu.VMEM((experts, room, width), bf16),
+            pltpu.VMEM((experts, room, width), bf16),
+            DMA((4,)),
+            DMA((3,)),
+            DMA((3,)),
+            DMA((parts - 1, GROUP)),
+            DMA((parts - 1, GROUP)),
+            DMA((3,)),
+            DMA((3,)),
+            DMA((experts - 1,)),
+            DMA((experts - 1,)),
+            DMA((experts - 1,)),
+            DMA((experts - 1,)),
+        ],
+        compiler_params=pltpu.CompilerParams(
+            collective_id=layer, has_side_effects=True, vmem_limit_bytes=56 * 2**20
+        ),
+        name="layer_forward",
+    )(x, gains, w_router, select, chosen, bias, w_qkv, w_output, w_in, w_out)
+
+
+def bucket_blocks():
+    row = np.arange(BLOCK)[:, None]
+    column = np.arange(BLOCK)[None, :]
+    made = []
+    for offset in (-2, -1, 0, 1, 2):
+        r = offset * BLOCK + column - row
+        n = np.abs(r)
+        beyond = 8 + sum((n >= limit).astype(np.int32) for limit in thresholds)
+        made.append(np.where(n < 8, n, beyond) + np.where(r > 0, 16, 0))
+    return np.stack(made).astype(np.int32)
+
+
+def bias_blocks(rel_bias, first_head):
+    mine = lax.dynamic_slice_in_dim(rel_bias, first_head, 3, 1)
+    buckets = jnp.asarray(bucket_blocks())
+    made = jnp.zeros((3,) + buckets.shape, f32)
+    for bucket in range(rel_bias.shape[0]):
+        made = jnp.where(buckets[None] == bucket, mine[bucket][:, None, None, None], made)
+    return made
+
+
+def swap_route():
+    d, c, e = (lax.axis_size(name) for name in ("dp", "context", "expert"))
+    return [((i * c + j) * e + k, (k * c + j) * e + i) for i in range(d) for j in range(c) for k in range(e)]
+
+
+def swapped(block):
+    return lax.ppermute(block, ("dp", "context", "expert"), swap_route())
+
+
+def routing(routes, kept, experts, room):
+    layers, count = routes.shape
+    chosen = (routes[..., None] == lax.iota(jnp.int32, experts)).astype(jnp.int32)
+    rank = jnp.sum(chosen * (jnp.cumsum(chosen, axis=1) - 1), axis=-1)
+    target = routes * room + rank
+    slot = lax.iota(jnp.int32, experts * room)[None, :, None]
+    select = ((slot == target[:, None, :]) & (kept[:, None, :] > 0)).astype(bf16)
+    live = ((routes[..., None] == lax.iota(jnp.int32, 128)) & (kept[..., None] > 0)).astype(f32)
+    return select.reshape(layers, experts, room, count), live
+
+
+def forward_path(tokens, w_query, w_key, w_value, w_output, rel_bias, gain_attn, gain_moe, w_router, w_in, w_out, routes, kept):
+    batch, count, width = tokens.shape
+    experts = w_router.shape[2]
+    room = count * 5 // (4 * experts)
+    layers = w_query.shape[0]
+    block = 2 * (lax.axis_index("context") % 2) + lax.axis_index("dp") // 2
+    x = swapped(tokens[0]).astype(f32)
+    marks = swapped(jnp.stack([routes[:, 0, :, 0], kept[:, 0, :]]))
+    select, chosen = routing(marks[0], marks[1], experts, room)
+    bias = bias_blocks(rel_bias, 3 * block)
+    wide = 3 * HEAD
+    w_qkv = jnp.concatenate(
+        [lax.dynamic_slice_in_dim(w, wide * block, wide, 2) for w in (w_key, w_value, w_query)], axis=2
+    )
+    router_wide = jnp.pad(w_router, ((0, 0), (0, 0), (0, 128 - experts)))
+    for layer in range(layers):
+        gains = jnp.stack([gain_attn[layer], gain_moe[layer]])
+        saved = forward_layer(layer, x, gains, router_wide[layer], select[layer], chosen[layer], bias, w_qkv, w_output, w_in, w_out)
+        x = saved[-1]
+    return swapped(x.astype(bf16))[None]
 
 
 def passed_along(block, axis, distance):
@@ -465,6 +934,9 @@
         ).astype(jnp.float32),
     )
     bias_out = lax.psum(table_grad, ("dp", "context", "expert"))
+    output = forward_path(
+        tokens, w_query, w_key, w_value, w_output, rel_bias, gain_attn, gain_moe, w_router, w_in, w_out, routes, kept
+    )
     return (
         output,
         grad.reshape(batch, count, width),

time: 1250 us -> 1270 us (1.016)
  waiting for transfers between devices: 682 us -> 557 us
  Pallas kernels: 0 us -> 105 us
  other arithmetic: 75.6 us -> 90.9 us
    pallas_call x0 -> x2, Pallas kernels: none -> 105 us  [forward_layer(): pl.pallas_call(functools.partial(forward_kernel, layer, parts, experts),...]
    reduce_scatter x1, waiting for transfers between devices: 110 us -> 35.1 us  [on_device(): lax.psum_scatter(jnp.stack(query_list), ('dp', 'context', 'expert'), scat...]
    reduce_scatter x1, waiting for transfers between devices: 52.8 us -> 0.01 us  [on_device(): lax.psum_scatter(jnp.stack(out_list).astype(jnp.bfloat16), ('dp', 'contex...]
    all_gather x2, waiting for transfers between devices: 46.8 us -> 75 us  [on_device(): lax.all_gather(jnp.stack([keys, values]), 'expert', axis=2, tiled=True)]
    ppermute x2, waiting for transfers between devices: 42.8 us -> 17.6 us  [passed_along(): return lax.ppermute(block, axis, route)]
    unnamed x352 -> x436, local copies, waits for them, and re-layouts: 127 us -> 129 us
  transfers between devices with their start and end apart: 17 -> 20, of which waited for: 15 -> 13; matrix products, arithmetic and copies ran while one was open for 16% -> 17% of each run, Pallas kernels for 0% -> 8%
where the time goes in v1:
time: 1270 us; the launch traced here: 1260 us
  waiting for transfers between devices  557 us (44%)
  local copies, waits for them, and re-layouts  226 us (18%)
  matrix products  153 us (12%)
  Pallas kernels  105 us (8%)
  other arithmetic  90.9 us (7%)
  blocking collectives  83.3 us (7%)
  starting transfers between devices  29.2 us (2%)
  between operations  17.4 us (1%)
    unnamed x436, local copies, waits for them, and re-layouts  129 us
    reduce_scatter x1, waiting for transfers between devices, on_device(): lax.psum_scatter(jnp.stack(output_list), ('dp', 'context', 'expert'), sca...  113 us
    reduce_scatter x1, waiting for transfers between devices, on_device(): lax.psum_scatter(jnp.stack(value_list), ('dp', 'context', 'expert'), scat...  113 us
    reduce_scatter x1, waiting for transfers between devices, on_device(): lax.psum_scatter(jnp.stack(key_list), ('dp', 'context', 'expert'), scatte...  112 us
    pallas_call x2, Pallas kernels, forward_layer(): pl.pallas_call(functools.partial(forward_kernel, layer, parts, experts),...  105 us
    all_gather x2, waiting for transfers between devices, on_device(): lax.all_gather(jnp.stack([keys, values]), 'expert', axis=2, tiled=True)  75 us
    unnamed x12, waiting for transfers between devices  69.4 us
    psum x1, blocking collectives, on_device(): bias_out = lax.psum(table_grad, ('dp', 'context', 'expert'))  52.3 us
  transfers between devices with their start and end apart: 20, of which 13 were waited for; matrix products, arithmetic and copies ran while one was open for 17% of the time, Pallas kernels for 8%

profile of v1, /device:TPU:0, one launch (start us, length us, event | category | flops | bytes accessed | tf_op | source)
XLA Modules:
  0.0 1261.9 jit_solution(15219795952589625783)
XLA Ops:
  15.8 38.9 %all-gather.3.cloned.1.call-done = bf16[2,1,512,768]{3,2,1,0:T(8,128)(2,1)} async-done(((bf16[2,1,128,768]{3,2,1,0:T(8,128)(2,1)}), bf16[2,1,512,768]{3,2,1,0:T(8,128)(2,1)}) %all-gather.3.cloned.1.call-update) | async-done | bytes 1572880 | tf_op jit(solution)/shard_map/all_gather | solution.py:708
  63.0 7.1 reshape.1480
  76.7 7.4 reshape.1483
  97.0 5.2 fusion.404
  123.8 6.1 all-to-all-done
  156.3 36.0 %all-gather.5.cloned.1.call-done = bf16[2,1,512,768]{3,2,1,0:T(8,128)(2,1)} async-done(((bf16[2,1,128,768]{3,2,1,0:T(8,128)(2,1)}), bf16[2,1,512,768]{3,2,1,0:T(8,128)(2,1)}) %all-gather.5.cloned.1.call-update) | async-done | bytes 1572880 | tf_op jit(solution)/shard_map/all_gather | solution.py:708
  205.2 5.8 fusion.406
  211.0 17.6 %collective-permute-done.4 = bf16[2,1,512,768]{3,2,1,0:T(8,128)(2,1)} collective-permute-done((bf16[2,1,512,768]{3,2,1,0:T(8,128)(2,1)}, bf16[2,1,512,768]{3,2,1,0:T(8,128)(2,1)}, u32[]{:S(2)}, u32[]{:S(2)}) %collective-permute-start.4) | collective-permute-done | bytes 1572896 | tf_op jit(solution)/shard_map/while/body/eval_jaxpr/ppermute | solution.py:483
  233.6 5.4 fusion.407
  254.9 10.2 all_to_all.40
  288.9 10.2 all_to_all.41
  299.1 5.1 fusion.89
  344.5 15.8 %copy.110 = bf16[2,1,1024,768]{3,1,0,2:T(2,128)(2,1)} copy(bf16[2,1,1024,768]{2,3,1,0:T(8,128)(2,1)} %maximum_dynamic-update-slice_fusion.1) | data formatting | bytes 6291456
  360.3 22.3 %bitcast_reduce_fusion.1 = bf16[1024,2,768]{2,1,0:T(2,128)(2,1)S(1)} fusion(bf16[2,1,1024,768]{3,1,0,2:T(2,128)(2,1)} %copy.110), kind=kLoop, calls=%fused_computation.7 | loop fusion | bytes 6291456
  390.0 69.3 %reduce-scatter.28.cloned.1.call-done = bf16[128,1536]{1,0:T(8,128)(2,1)} async-done(((bf16[1024,1536]{1,0:T(8,128)(2,1)}), bf16[128,1536]{1,0:T(8,128)(2,1)}) %reduce-scatter.28.cloned.1.call-update) | async-done | bytes 393232
  472.6 10.7 all_to_all.42
  483.2 5.2 fusion.84
  520.2 11.6 copy.112
  531.8 22.3 %bitcast_reduce_fusion = bf16[1024,2,768]{2,1,0:T(2,128)(2,1)S(1)} fusion(bf16[2,1,1024,768]{3,1,0,2:T(2,128)(2,1)} %copy.112), kind=kLoop, calls=%fused_computation.6 | loop fusion | bytes 6291456
  565.9 8.3 pad_maximum_fusion
  575.1 5.6 fusion.19
  584.8 8.4 pad_maximum_fusion.1
  612.9 49.4 %layer_forward.2 = (bf16[4,128,768]{2,1,0:T(8,128)(2,1)}, bf16[4,128,192]{2,1,0:T(8,128)(2,1)}, bf16[2,4,128,384]{3,2,1,0:T(8,128)(2,1)}, f32[4,128,192]{2,1,0:T...) custom-call(f32[128,768]{1,0:T(8,128)} %convert_element_type.643.x, ...), custom_call_target="tpu_custom_call" | custom-call | tf_op jit(solution)/shard_map/layer_forward/pallas_call | solution.py:369
  662.3 55.8 %layer_forward.3 = (bf16[4,128,768]{2,1,0:T(8,128)(2,1)}, bf16[4,128,192]{2,1,0:T(8,128)(2,1)}, bf16[2,4,128,384]{3,2,1,0:T(8,128)(2,1)}, f32[4,128,192]{2,1,0:T...) custom-call(f32[128,768]{1,0:T(8,128)} %get-tuple-element.104.x, ...), custom_call_target="tpu_custom_call" | custom-call | tf_op jit(solution)/shard_map/layer_forward/pallas_call | solution.py:369
  729.6 6.8 reshape.1515
  777.9 5.6 reshape.1521
  783.5 6.5 reshape.1524
  818.7 52.3 %all-reduce.12 = (f32[32,12]{0,1:T(8,128)}, f32[2,768]{1,0:T(2,128)S(1)}, f32[2,768]{1,0:T(2,128)S(1)}, f32[2,768,4]{1,2,0:T(4,128)S(1)}) all-reduce(f32[32,12]{0,1:T(8,128)S(1)} %fusion.217, f32[2,768]{1,0:T(2,128)S(1)} %pad_maximum_fusion.12, ...), channel_id=1, replica_groups=mesh['dp'=4,'context'=2,'expert'=4] {'dp','context','expert'}, use_global_device_ids=true, to_apply=%region_42.43 | all-reduce | flops 9600 | bytes 76800 | tf_op jit(solution)/shard_map/psum | solution.py:936
  879.7 35.1 %reduce-scatter.16.cloned.1.call-done = f32[2,24,768]{2,1,0:T(8,128)} async-done(((f32[2,768,768]{2,1,0:T(8,128)}), f32[2,24,768]{2,1,0:T(8,128)}) %reduce-scatter.16.cloned.1.call-update) | async-done | bytes 147472 | tf_op jit(solution)/shard_map/reduce_scatter | solution.py:900
  914.8 113.2 %reduce-scatter.22.cloned.1.call-done = f32[2,24,768]{2,1,0:T(8,128)} async-done(((f32[2,768,768]{2,1,0:T(8,128)}), f32[2,24,768]{2,1,0:T(8,128)}) %reduce-scatter.22.cloned.1.call-update) | async-done | bytes 147472 | tf_op jit(solution)/shard_map/reduce_scatter | solution.py:909
  1028.0 112.2 %reduce-scatter.18.cloned.1.call-done = f32[2,24,768]{2,1,0:T(8,128)} async-done(((f32[2,768,768]{2,1,0:T(8,128)}), f32[2,24,768]{2,1,0:T(8,128)}) %reduce-scatter.18.cloned.1.call-update) | async-done | bytes 147472 | tf_op jit(solution)/shard_map/reduce_scatter | solution.py:903
  1140.2 113.0 %reduce-scatter.20.cloned.1.call-done = f32[2,24,768]{2,1,0:T(8,128)} async-done(((f32[2,768,768]{2,1,0:T(8,128)}), f32[2,24,768]{2,1,0:T(8,128)}) %reduce-scatter.20.cloned.1.call-update) | async-done | bytes 147472 | tf_op jit(solution)/shard_map/reduce_scatter | solution.py:906
  (680 shorter events, 360.0 us)
Async XLA Ops:
  7.2 47.5 %all-gather.3.cloned.1.call-start = ((), (), s32[]{:S(2)}) async-start(), calls=%async_computation.16 | async-start | bytes 1966080 | tf_op jit(solution)/shard_map/all_gather | solution.py:708
  14.8 39.9 %copy-start.178 = (s32[640]{0:T(1024)}, s32[640]{0:T(1024)S(1)}, u32[]{:S(2)}) copy-start(s32[640]{0:T(1024)S(1)} %fusion.346) | copy-start | bytes 7684
  14.9 42.0 %copy-start.175 = (s32[640]{0:T(1024)}, s32[640]{0:T(1024)S(1)}, u32[]{:S(2)}) copy-start(s32[640]{0:T(1024)S(1)} %fusion.347) | copy-start | bytes 7684
  14.9 69.7 %copy-start.138 = (s32[128]{0:T(128)}, s32[128]{0:T(128)S(1)}, u32[]{:S(2)}) copy-start(s32[128]{0:T(128)S(1)} %get-tuple-element.235) | copy-start | bytes 1540
  14.9 69.6 %copy-start.140 = (s32[128]{0:T(128)}, s32[128]{0:T(128)S(1)}, u32[]{:S(2)}) copy-start(s32[128]{0:T(128)S(1)} %get-tuple-element.234) | copy-start | bytes 1540
  54.7 37.3 %collective-permute-start.3 = (bf16[2,1,512,768]{3,2,1,0:T(8,128)(2,1)}, bf16[2,1,512,768]{3,2,1,0:T(8,128)(2,1)}, u32[]{:S(2)}, u32[]{:S(2)}) collective-permute-start(bf16[2,1,512,768]{3,2,1,0:T(8,128)(2,1)} %all-gather.3.cloned.1.call-done), channel_id=1, source_target_pairs={{4,0},{0,4},{5,1},{1,5},{6,2},{2,6},{7,3},{3,7},{12,8},{8,12},{13,... | collective-permute-start | bytes 4718600 | tf_op jit(solution)/shard_map/while/body/eval_jaxpr/ppermute | solution.py:483
  70.3 26.7 %copy-start.53 = (bf16[128,768]{0,1:T(8,128)(2,1)}, bf16[128,768]{0,1:T(8,128)(2,1)S(1)}, u32[]{:S(2)}) copy-start(bf16[128,768]{0,1:T(8,128)(2,1)S(1)} %copy.82) | copy-start | bytes 589828
  117.4 12.5 all-to-all-start
  139.0 10.8 all-to-all-start.1
  143.1 49.3 %all-gather.5.cloned.1.call-start = ((), (), s32[]{:S(2)}) async-start(), calls=%async_computation.17 | async-start | bytes 1966080 | tf_op jit(solution)/shard_map/all_gather | solution.py:708
  192.3 36.3 %collective-permute-start.4 = (bf16[2,1,512,768]{3,2,1,0:T(8,128)(2,1)}, bf16[2,1,512,768]{3,2,1,0:T(8,128)(2,1)}, u32[]{:S(2)}, u32[]{:S(2)}) collective-permute-start(bf16[2,1,512,768]{3,2,1,0:T(8,128)(2,1)} %all-gather.5.cloned.1.call-done), channel_id=1, source_target_pairs={{4,0},{0,4},{5,1},{1,5},{6,2},{2,6},{7,3},{3,7},{12,8},{8,12},{13,... | collective-permute-start | bytes 4718600 | tf_op jit(solution)/shard_map/while/body/eval_jaxpr/ppermute | solution.py:483
  250.6 19.2 %slice-start.3 = ((s8[9437184]{0:T(1024)(128)(4,1)}), s8[1048576]{0:T(1024)(128)(4,1)S(1)}, s32[]{:S(2)}) async-start(s8[9437184]{0:T(1024)(128)(4,1)} %bitcast.691), calls=%async_computation.29 | async-start | bytes 2097152
  271.9 11.2 all-to-all-start.5
  309.9 10.8 all-to-all-start.4
  314.0 145.3 %reduce-scatter.28.cloned.1.call-start = ((), (), s32[]{:S(2)}) async-start(), calls=%async_computation.24 | async-start | bytes 3538944
  467.9 21.6 %slice-start = ((s8[9437184]{0:T(1024)(128)(4,1)}), s8[4194304]{0:T(1024)(128)(4,1)S(1)}, s32[]{:S(2)}) async-start(s8[9437184]{0:T(1024)(128)(4,1)} %bitcast.689), calls=%async_computation.26 | async-start | bytes 8388608
  491.9 10.8 all-to-all-start.7
  495.9 294.1 %reduce-scatter.30.cloned.1.call-start = ((), (), s32[]{:S(2)}) async-start(), calls=%async_computation.25 | async-start | bytes 3538944
  556.4 317.5 %reduce-scatter.24.cloned.1.call-start = ((), (), s32[]{:S(2)}) async-start(), calls=%async_computation.22 | async-start | bytes 10616832 | tf_op jit(solution)/shard_map/reduce_scatter | solution.py:923
  574.2 302.6 %reduce-scatter.26.cloned.1.call-start = ((), (), s32[]{:S(2)}) async-start(), calls=%async_computation.23 | async-start | bytes 10616832 | tf_op jit(solution)/shard_map/reduce_scatter | solution.py:929
  593.2 321.6 %reduce-scatter.16.cloned.1.call-start = ((), (), s32[]{:S(2)}) async-start(), calls=%async_computation.18 | async-start | bytes 4866048 | tf_op jit(solution)/shard_map/reduce_scatter | solution.py:900
  594.1 18.0 %collective-permute-start = (bf16[128,768]{1,0:T(8,128)(2,1)S(1)}, bf16[128,768]{1,0:T(8,128)(2,1)S(1)}, u32[]{:S(2)}, u32[]{:S(2)}) collective-permute-start(bf16[128,768]{1,0:T(8,128)(2,1)S(1)} %bitcast.737), channel_id=1, source_target_pairs={{0,0},{1,8},{2,16},{3,24},{4,4},{5,12},{6,20},{7,28},{8,1},{9,9},{... | collective-permute-start | bytes 589832 | tf_op jit(solution)/shard_map/ppermute | solution.py:444
  594.8 15.3 %collective-permute-start.1 = (s32[2,2,128]{2,1,0:T(2,128)S(1)}, s32[2,2,128]{2,1,0:T(2,128)S(1)}, u32[]{:S(2)}, u32[]{:S(2)}) collective-permute-start(s32[2,2,128]{2,1,0:T(2,128)S(1)} %pad_add_fusion), channel_id=1, source_target_pairs={{0,0},{1,8},{2,16},{3,24},{4,4},{5,12},{6,20},{7,28},{8,1},{9,9},{... | collective-permute-start | bytes 6152 | tf_op jit(solution)/shard_map/ppermute | solution.py:444
  662.3 60.8 %copy-start.89 = (f32[768]{0:T(1024)S(1)}, f32[768]{0:T(1024)}, u32[]{:S(2)}) copy-start(f32[768]{0:T(1024)} %get-tuple-element.126) | copy-start | bytes 9220
  662.3 60.8 %copy-start.141 = (s32[128]{0:T(128)S(1)}, s32[128]{0:T(128)}, u32[]{:S(2)}) copy-start(s32[128]{0:T(128)} %copy-done.140) | copy-start | bytes 1540
  662.3 62.8 %copy-start.18 = (bf16[12,128,512]{2,1,0:T(8,128)(2,1)S(1)}, bf16[12,128,512]{2,1,0:T(8,128)(2,1)}, u32[]{:S(2)}) copy-start(bf16[12,128,512]{2,1,0:T(8,128)(2,1)} %copy-done.17) | copy-start | bytes 4718596
  719.9 3.2 collective-permute-start.2
  750.8 277.2 %reduce-scatter.22.cloned.1.call-start = ((), (), s32[]{:S(2)}) async-start(), calls=%async_computation.21 | async-start | bytes 4866048 | tf_op jit(solution)/shard_map/reduce_scatter | solution.py:909
  759.5 380.7 %reduce-scatter.18.cloned.1.call-start = ((), (), s32[]{:S(2)}) async-start(), calls=%async_computation.19 | async-start | bytes 4866048 | tf_op jit(solution)/shard_map/reduce_scatter | solution.py:903
  801.7 451.4 %reduce-scatter.20.cloned.1.call-start = ((), (), s32[]{:S(2)}) async-start(), calls=%async_computation.20 | async-start | bytes 4866048 | tf_op jit(solution)/shard_map/reduce_scatter | solution.py:906
  817.2 55.8 %copy-start.185 = (f32[128]{0:T(128)S(1)}, f32[128]{0:T(128)}, u32[]{:S(2)}) copy-start(f32[128]{0:T(128)} %copy-done.184) | copy-start | bytes 1540
  817.2 55.8 %copy-start.49 = (f32[128,768]{1,0:T(8,128)S(1)}, f32[128,768]{1,0:T(8,128)}, u32[]{:S(2)}) copy-start(f32[128,768]{1,0:T(8,128)} %copy-done.47) | copy-start | bytes 1179652
  (194 other events, 612.2 us)
Sparse Core Ops, SparseCore 0:
  14.9 39.7 all-gather.2
  156.4 35.8 all-gather.4
  385.0 74.2 reduce-scatter.27
  556.5 74.5 reduce-scatter.29
  634.4 86.8 reduce-scatter.23
  724.6 76.4 reduce-scatter.25
  807.2 107.6 reduce-scatter.15
  921.8 106.1 reduce-scatter.21
  1034.1 106.0 reduce-scatter.17
  1147.0 106.1 reduce-scatter.19
